TPU v7x, 128 devices: a whole 4x4x4 slice. The times are simulated.
128 devices in a mesh: cand: 8 (over x_hi, z), prompt: 16 (over x_lo, y, core).
Axes of the slice: x: 4 (x_hi: 2, x_lo: 2; x = x_hi * 2 + x_lo), y: 4, z: 4, core: 2. Of those that a mesh axis runs over, the one named last changes fastest.
Arguments:
- hidden_states: bfloat16 [16, 8, 128, 4096], P('prompt', 'cand'), may hold values from -8 to 8
- proj_weight: bfloat16 [4096, 1024], P(('cand', 'prompt')), may hold values from -0.0625 to 0.0625
- bilinear: bfloat16 [1024, 1024], P(('cand', 'prompt')), may hold values from -0.005859375 to 0.005859375
- lengths: int32 [16, 8], P('prompt'), may hold values from 32 to 128, as said below
- labels: int32 [16, 28], P('prompt'), may hold values 0 or 1
Outputs:
- pair_logits: float32 [16, 8, 8], P('prompt')
- grad_proj: float32 [4096, 1024], P(('cand', 'prompt'))
- grad_bilinear: float32 [1024, 1024], P(('cand', 'prompt'))
Inputs may be any that keep to these rules, and one draw needn't show every extreme that they name: `lengths`: every prompt has a candidate with all 128 rows valid.
All inputs are finite; a program needn't handle non-finite values. No bound on the sum of `labels` on one device may be relied on, other than what follows from the above.
Results may differ from a plain program's by a relative error of at most 0.0045.
Values may be sent and summed in bfloat16 or wider, within the bound.
No kernel may reach another device: no remote copies, remote signals or barrier semaphores. Data moves between devices by JAX's collectives and lax.ppermute only.
A program may use at most 128 MiB of HBM per device.

v0:
```python
import jax
import jax.numpy as jnp
import numpy as np
from jax import lax
from jax.sharding import PartitionSpec as P

HEADS = 16
HEAD_DIM = 64
EPSILON = 1e-06
HIGH = lax.Precision.HIGHEST


def shifted_2(value, axis, steps):
    count = lax.axis_size(axis)
    pairs = [(source, (source + steps) % count) for source in range(count)]
    return lax.ppermute(value, axis, pairs)


def attend_block(queries, keys, key_valid, factor):
    prompts, rows, width = queries.shape
    query_heads = queries.reshape(prompts, rows, HEADS, HEAD_DIM)
    key_heads = keys.reshape(prompts, rows, HEADS, HEAD_DIM)
    scores = (
        jnp.einsum("pthd,pshd->phts", query_heads, key_heads, preferred_element_type=jnp.float32)
        * factor
    )
    scores = jnp.where(key_valid[:, None, None, :], scores, -jnp.inf)
    shifted = jnp.exp(scores - jnp.max(scores, axis=3, keepdims=True))
    weights = shifted / jnp.sum(shifted, axis=3, keepdims=True)
    mixed = jnp.einsum(
        "phts,pshd->pthd",
        weights.astype(jnp.bfloat16),
        key_heads,
        preferred_element_type=jnp.float32,
    )
    return (weights, mixed)


def body(hidden_states, proj_weight, bilinear, lengths, labels):
    cands = lax.axis_size("cand")
    here = lax.axis_index("cand")
    prompts = hidden_states.shape[0]
    rows = hidden_states.shape[2]
    width = hidden_states.shape[3]
    inner = proj_weight.shape[1]
    factor = HEAD_DIM ** (-0.5)
    flat = hidden_states.reshape(prompts * rows, width)
    columns = flat
    projected = jnp.dot(
        columns,
        lax.all_gather(proj_weight, ("cand", "prompt"), axis=0, tiled=True),
        preferred_element_type=jnp.float32,
    )
    own_rows = projected.astype(jnp.bfloat16).reshape(prompts, rows, inner)
    own_heads = own_rows.reshape(prompts, rows, HEADS, HEAD_DIM)
    cand_ids = jnp.arange(cands, dtype=jnp.int32)
    positions = jnp.arange(rows, dtype=jnp.int32)

    def length_of(source):
        return jnp.sum(jnp.where(cand_ids[None, :] == source, lengths, 0), axis=1)

    own_length = length_of(here)
    own_valid = positions[None, :] < own_length[:, None]
    own_length_f = own_length.astype(jnp.float32)
    received = {}
    moving = own_rows
    for offset in range(1, cands):
        moving = shifted_2(moving, "cand", 1)
        received[offset] = moving
    sources = {}
    means = {}
    radii = {}
    pooled = jnp.zeros((prompts, cands, inner), jnp.float32)
    for offset in range(1, cands):
        source = (here - offset) % cands
        other_valid = positions[None, :] < length_of(source)[:, None]
        weights, mixed = attend_block(own_rows, received[offset], other_valid, factor)
        total = jnp.sum(jnp.where(own_valid[:, :, None, None], mixed, 0.0), axis=1)
        mean_row = total.reshape(prompts, inner) / own_length_f[:, None]
        radius = jnp.sqrt(jnp.mean(mean_row * mean_row, axis=1, keepdims=True) + EPSILON)
        normed = mean_row / radius
        pooled = pooled + jnp.where((cand_ids == source)[None, :, None], normed[:, None, :], 0.0)
        sources[offset] = source
        means[offset] = mean_row
        radii[offset] = radius
    everything = lax.all_gather(pooled[:, None], "cand", axis=1, tiled=True)
    full_bil = lax.all_gather(bilinear, ("cand", "prompt"), axis=0, tiled=True).astype(jnp.float32)
    toward = jnp.einsum("ab,pjib->pija", full_bil, everything, precision=HIGH)
    pair_logits = jnp.sum(everything * toward, axis=3)
    upper_i, upper_j = np.triu_indices(cands, 1)
    wins = labels.astype(jnp.float32)
    target = (
        jnp.zeros((prompts, cands, cands), jnp.float32)
        .at[:, upper_i, upper_j]
        .set(wins)
        .at[:, upper_j, upper_i]
        .set(1.0 - wins)
    )
    offdiag = 1.0 - jnp.eye(cands, dtype=jnp.float32)
    sign = 2.0 * target - 1.0
    dlogit = -sign * jax.nn.sigmoid(-sign * pair_logits) * offdiag[None]
    backward_dir = jnp.einsum("ba,pjib->pija", full_bil, everything, precision=HIGH)
    dpooled = dlogit[..., None] * toward + jnp.swapaxes(dlogit, 1, 2)[..., None] * backward_dir
    own_mask = cand_ids == here
    dnormed_own = jnp.sum(jnp.where(own_mask[None, :, None, None], dpooled, 0.0), axis=1)
    reverse_pool = jnp.sum(jnp.where(own_mask[None, None, :, None], everything, 0.0), axis=2)
    own_dlogit = jnp.sum(jnp.where(own_mask[None, :, None], dlogit, 0.0), axis=1)
    bil_term = jnp.einsum("pj,pja,pjb->ab", own_dlogit, pooled, reverse_pool, precision=HIGH)
    grad_bilinear = lax.psum_scatter(bil_term, ("cand", "prompt"), scatter_dimension=0, tiled=True)
    row_weight = jnp.where(own_valid, 1.0, 0.0) / own_length_f[:, None]
    query_grads = jnp.zeros((prompts, rows, inner), jnp.float32)
    owners = jnp.zeros((cands, prompts, rows, inner), jnp.float32)
    for offset in range(1, cands):
        backward_source = sources[offset]
        others = received[offset]
        backward_other_valid = positions[None, :] < length_of(backward_source)[:, None]
        backward_weights, unused = attend_block(own_rows, others, backward_other_valid, factor)
        dnorm = jnp.sum(
            jnp.where((cand_ids == backward_source)[None, :, None], dnormed_own, 0.0), axis=1
        )
        norm_row = means[offset] / radii[offset]
        dmean = (dnorm - norm_row * jnp.mean(dnorm * norm_row, axis=1, keepdims=True)) / radii[
            offset
        ]
        dmean_heads = dmean.reshape(prompts, HEADS, HEAD_DIM)
        other_heads = others.reshape(prompts, rows, HEADS, HEAD_DIM)
        along = jnp.einsum(
            "pshd,phd->phs", other_heads.astype(jnp.float32), dmean_heads, precision=HIGH
        )
        expected = jnp.einsum("phts,phs->pht", backward_weights, along, precision=HIGH)
        dscore = (
            row_weight[:, None, :, None]
            * backward_weights
            * (along[:, :, None, :] - expected[:, :, :, None])
            * factor
        )
        dscore = dscore.astype(jnp.bfloat16)
        dquery = jnp.einsum(
            "phts,pshd->pthd", dscore, other_heads, preferred_element_type=jnp.float32
        )
        column = jnp.einsum("phts,pt->phs", backward_weights, row_weight, precision=HIGH)
        dkey = jnp.einsum(
            "phts,pthd->pshd", dscore, own_heads, preferred_element_type=jnp.float32
        ) + jnp.einsum("phs,phd->pshd", column, dmean_heads, precision=HIGH)
        dquery, dkey, source = (
            dquery.reshape(prompts, rows, inner),
            dkey.reshape(prompts, rows, inner),
            backward_source,
        )
        query_grads = query_grads + dquery
        owners = owners + jnp.where((cand_ids == source)[:, None, None, None], dkey[None], 0.0)
    home = lax.psum_scatter(owners, "cand", scatter_dimension=0, tiled=True)[0]
    total_grad = (query_grads + home).astype(jnp.bfloat16).reshape(prompts * rows, inner)
    columns = flat
    grad_proj = lax.psum_scatter(
        lax.dot_general(
            columns, total_grad, (((0,), (0,)), ((), ())), preferred_element_type=jnp.float32
        ),
        ("cand", "prompt"),
        scatter_dimension=0,
        tiled=True,
    )
    return (pair_logits, grad_proj, grad_bilinear)


def solution(mesh):
    in_specs = (
        P("prompt", "cand", None, None),
        P(("cand", "prompt"), None),
        P(("cand", "prompt"), None),
        P("prompt", None),
        P("prompt", None),
    )
    out_specs = (P("prompt", None, None), P(("cand", "prompt"), None), P(("cand", "prompt"), None))
    return jax.shard_map(body, mesh=mesh, in_specs=in_specs, out_specs=out_specs, check_vma=False)
```

profile of v0, /device:TPU:0, one launch (start us, length us, event | category | flops | bytes accessed | tf_op | source)
XLA Modules:
  0.0 1861.5 jit_solution(6400430401243026478)
XLA Ops:
  18.1 197.4 %all-gather.3.cloned.1.call-done = bf16[4096,1024]{1,0:T(8,128)(2,1)} async-done(((bf16[32,1024]{1,0:T(8,128)(2,1)}), bf16[4096,1024]{1,0:T(8,128)(2,1)}) %all-gather.3.cloned.1.call-update) | async-done | bytes 8388624 | tf_op jit(solution)/shard_map/all_gather | solution.py:51
  215.5 4.6 convolution_convert_fusion
  226.5 5.1 collective-permute-done
  235.9 8.7 collective-permute-done.1
  249.1 9.9 collective-permute-done.2
  267.2 3.0 fusion.144
  270.1 7.4 collective-permute-done.3
  283.1 10.1 collective-permute-done.4
  300.9 3.0 fusion.140
  303.8 7.4 collective-permute-done.5
  316.8 6.8 collective-permute-done.6
  331.3 36.6 %all_gather.10 = f32[1,8,8,1024]{3,2,0,1:T(8,128)} all-gather(f32[1,1,8,1024]{3,2,0,1:T(8,128)S(1)} %select_add_fusion.1), channel_id=1, replica_groups=mesh['cand'=8,'prompt'=16] {'cand'}, dimensions={1}, use_global_device_ids=true | all-gather | bytes 294912 | tf_op jit(solution)/shard_map/all_gather | solution.py:86
  368.0 3.0 fusion.136
  370.9 48.1 %all-gather.5.cloned.1.call-done = bf16[1024,1024]{1,0:T(8,128)(2,1)} async-done(((bf16[8,1024]{1,0:T(8,128)(2,1)}), bf16[1024,1024]{1,0:T(8,128)(2,1)}) %all-gather.5.cloned.1.call-update) | async-done | bytes 2097168 | tf_op jit(solution)/shard_map/all_gather | solution.py:87
  419.0 4.4 select_reduce_fusion
  424.1 2.9 fusion.40
  442.8 2.5 fusion.108
  460.4 5.0 select_add_fusion
  465.4 5.8 fusion.77
  477.9 70.6 %reduce-scatter.6.cloned.1.call-done = f32[1,1,128,1024]{2,3,1,0:T(8,128)} async-done(((f32[8,1,128,1024]{2,3,1,0:T(8,128)}), f32[1,1,128,1024]{2,3,1,0:T(8,128)}) %reduce-scatter.6.cloned.1.call-update) | async-done | bytes 524304 | tf_op jit(solution)/shard_map/reduce_scatter | solution.py:152
  548.5 9.1 convolution_bitcast_fusion
  557.6 17.5 copy.271
  575.1 617.9 %reduce-scatter.8.cloned.1.call-done = f32[8,1024]{1,0:T(8,128)} async-done(((f32[1024,1024]{1,0:T(8,128)}), f32[8,1024]{1,0:T(8,128)}) %reduce-scatter.8.cloned.1.call-update) | async-done | bytes 32784 | tf_op jit(solution)/shard_map/reduce_scatter | solution.py:109
  1193.0 661.6 %reduce-scatter.10.cloned.1.call-done = f32[32,1024]{1,0:T(8,128)} async-done(((f32[4096,1024]{1,0:T(8,128)}), f32[32,1024]{1,0:T(8,128)}) %reduce-scatter.10.cloned.1.call-update) | async-done | bytes 131088
  (413 shorter events, 87.5 us)
Async XLA Ops:
  7.2 208.3 %copy-start = (bf16[1,1,128,4096]{3,2,1,0:T(8,128)(2,1)S(1)}, bf16[1,1,128,4096]{3,2,1,0:T(8,128)(2,1)}, u32[]{:S(2)}) copy-start(bf16[1,1,128,4096]{3,2,1,0:T(8,128)(2,1)} %param.11) | copy-start | bytes 3145732
  7.2 208.3 %all-gather.3.cloned.1.call-start = ((), (), s32[]{:S(2)}) async-start(), calls=%async_computation.3 | async-start | bytes 8454144 | tf_op jit(solution)/shard_map/all_gather | solution.py:51
  7.9 411.1 %all-gather.5.cloned.1.call-start = ((), (), s32[]{:S(2)}) async-start(), calls=%async_computation.4 | async-start | bytes 2113536 | tf_op jit(solution)/shard_map/all_gather | solution.py:87
  8.7 539.8 %reduce-scatter.6.cloned.1.call-start = ((), (), s32[]{:S(2)}) async-start(), calls=%async_computation.5 | async-start | bytes 4718592 | tf_op jit(solution)/shard_map/reduce_scatter | solution.py:152
  10.2 321.0 %copy-start.90 = (pred[8]{0:T(512)(128)(4,1)}, pred[8]{0:T(512)(128)(4,1)S(1)}, u32[]{:S(2)}) copy-start(pred[8]{0:T(512)(128)(4,1)S(1)} %iota_compare_fusion.16) | copy-start | bytes 28
  10.2 321.0 %copy-start.57 = (pred[8]{0:T(512)(128)(4,1)}, pred[8]{0:T(512)(128)(4,1)S(1)}, u32[]{:S(2)}) copy-start(pred[8]{0:T(512)(128)(4,1)S(1)} %get-tuple-element.62) | copy-start | bytes 28
  10.2 321.0 %copy-start.59 = (pred[8]{0:T(512)(128)(4,1)}, pred[8]{0:T(512)(128)(4,1)S(1)}, u32[]{:S(2)}) copy-start(pred[8]{0:T(512)(128)(4,1)S(1)} %get-tuple-element.63) | copy-start | bytes 28
  13.0 269.6 %copy-start.133 = (pred[128]{0:T(512)(128)(4,1)}, pred[128]{0:T(512)(128)(4,1)S(1)}, u32[]{:S(2)}) copy-start(pred[128]{0:T(512)(128)(4,1)S(1)} %iota_compare_fusion.15) | copy-start | bytes 388
  14.4 266.5 %copy-start.108 = (f32[128]{0:T(128)}, f32[128]{0:T(128)S(1)}, u32[]{:S(2)}) copy-start(f32[128]{0:T(128)S(1)} %select_divide_fusion) | copy-start | bytes 1540
  18.1 204.2 %copy-start.34 = (s32[28]{0:T(128)S(1)}, s32[28]{0:T(128)}, u32[]{:S(2)}) copy-start(s32[28]{0:T(128)} %constant.182) | copy-start | bytes 340
  18.1 206.2 %copy-start.33 = (s32[28]{0:T(128)S(1)}, s32[28]{0:T(128)}, u32[]{:S(2)}) copy-start(s32[28]{0:T(128)} %constant.194) | copy-start | bytes 340
  220.2 11.5 collective-permute-start
  226.3 104.9 %copy-start.61 = (pred[8]{0:T(512)(128)(4,1)}, pred[8]{0:T(512)(128)(4,1)S(1)}, u32[]{:S(2)}) copy-start(pred[8]{0:T(512)(128)(4,1)S(1)} %get-tuple-element.60) | copy-start | bytes 28
  226.3 104.9 %copy-start.63 = (pred[8]{0:T(512)(128)(4,1)}, pred[8]{0:T(512)(128)(4,1)S(1)}, u32[]{:S(2)}) copy-start(pred[8]{0:T(512)(128)(4,1)S(1)} %get-tuple-element.61) | copy-start | bytes 28
  226.4 104.9 %copy-start.65 = (pred[8]{0:T(512)(128)(4,1)}, pred[8]{0:T(512)(128)(4,1)S(1)}, u32[]{:S(2)}) copy-start(pred[8]{0:T(512)(128)(4,1)S(1)} %get-tuple-element.58) | copy-start | bytes 28
  226.4 104.9 %copy-start.67 = (pred[8]{0:T(512)(128)(4,1)}, pred[8]{0:T(512)(128)(4,1)S(1)}, u32[]{:S(2)}) copy-start(pred[8]{0:T(512)(128)(4,1)S(1)} %get-tuple-element.59) | copy-start | bytes 28
  234.0 10.6 collective-permute-start.1
  248.7 10.4 collective-permute-start.2
  266.4 11.1 collective-permute-start.3
  282.6 10.6 collective-permute-start.4
  300.6 10.6 collective-permute-start.5
  313.0 10.6 collective-permute-start.6
  465.4 727.7 %reduce-scatter.8.cloned.1.call-start = ((), (), s32[]{:S(2)}) async-start(), calls=%async_computation.6 | async-start | bytes 4227072 | tf_op jit(solution)/shard_map/reduce_scatter | solution.py:109
  471.4 1383.3 %reduce-scatter.10.cloned.1.call-start = ((), (), s32[]{:S(2)}) async-start(), calls=%async_computation.7 | async-start | bytes 16908288
  (124 other events, 536.9 us)
Sparse Core Ops, SparseCore 0:
  9.7 205.7 all-gather.2
  217.2 201.7 all-gather.4
  465.5 82.9 reduce-scatter.5
  551.4 641.5 reduce-scatter.7
  1195.8 658.7 reduce-scatter.9
where the time goes:
time: 1870 us; the launch traced here: 1860 us
  waiting for transfers between devices  1650 us (88%)
  matrix products  79.6 us (4%)
  local copies, waits for them, and re-layouts  39.8 us (2%)
  blocking collectives  36.6 us (2%)
  between operations  25.7 us (1%)
  other arithmetic  25.1 us (1%)
    unnamed x6, waiting for transfers between devices  663 us
    reduce_scatter x1, waiting for transfers between devices, body(): lax.psum_scatter(bil_term, ('cand', 'prompt'), scatter_dimension=0, tiled...  618 us
    all_gather x1, waiting for transfers between devices, body(): lax.all_gather(proj_weight, ('cand', 'prompt'), axis=0, tiled=True)  197 us
    reduce_scatter x1, waiting for transfers between devices, body(): home = lax.psum_scatter(owners, 'cand', scatter_dimension=0, tiled=True)[0]  70.6 us
    ppermute x7, waiting for transfers between devices, shifted_2(): return lax.ppermute(value, axis, pairs)  55.3 us
    all_gather x1, waiting for transfers between devices, body(): lax.all_gather(bilinear, ('cand', 'prompt'), axis=0, tiled=True)  48.1 us
  transfers between devices with their start and end apart: 12, of which 12 were waited for; matrix products, arithmetic and copies ran while one was open for 5% of the time, Pallas kernels for 0%

commit v1 on v0

--- a/solution.py
+++ b/solution.py
@@ -8,6 +8,14 @@
 HEAD_DIM = 64
 EPSILON = 1e-06
 HIGH = lax.Precision.HIGHEST
+
+
+def layers_all_return_all(v0, device_axis):
+    local_part = jax.lax.axis_size(device_axis)
+    frame_out = jnp.stack([v0] * local_part, axis=0)
+    wide_out = jax.lax.all_to_all(frame_out, device_axis, concat_axis=0, split_axis=0)
+    e_next = jnp.concatenate(wide_out, axis=0)
+    return e_next
 
 
 def shifted_2(value, axis, steps):
@@ -48,7 +56,7 @@
     columns = flat
     projected = jnp.dot(
         columns,
-        lax.all_gather(proj_weight, ("cand", "prompt"), axis=0, tiled=True),
+        layers_all_return_all(proj_weight, ("cand", "prompt")),
         preferred_element_type=jnp.float32,
     )
     own_rows = projected.astype(jnp.bfloat16).reshape(prompts, rows, inner)

time: 1870 us -> 1760 us (0.941)
  waiting for transfers between devices: 1650 us -> 1520 us
    all_gather x1 -> x0, waiting for transfers between devices: 197 us -> none  [body(): lax.all_gather(proj_weight, ('cand', 'prompt'), axis=0, tiled=True)]
    all_to_all x0 -> x1, waiting for transfers between devices: none -> 101 us  [layers_all_return_all(): jax.lax.all_to_all(frame_out, device_axis, concat_axis=0, split_axis=0)]
    all_gather x1, waiting for transfers between devices: 48.1 us -> 11.1 us  [body(): lax.all_gather(bilinear, ('cand', 'prompt'), axis=0, tiled=True)]
    unnamed x6 -> x5, waiting for transfers between devices: 663 us -> 664 us
  transfers between devices with their start and end apart: 12 -> 12, of which waited for: 12 -> 12; matrix products, arithmetic and copies ran while one was open for 5% -> 6% of each run, Pallas kernels for 0% -> 0%
where the time goes in v1:
time: 1760 us; the launch traced here: 1750 us
  waiting for transfers between devices  1520 us (86%)
  matrix products  79.7 us (5%)
  local copies, waits for them, and re-layouts  45.1 us (3%)
  blocking collectives  36.7 us (2%)
  between operations  26 us (1%)
  other arithmetic  23.1 us (1%)
    unnamed x5, waiting for transfers between devices  664 us
    reduce_scatter x1, waiting for transfers between devices, body(): lax.psum_scatter(bil_term, ('cand', 'prompt'), scatter_dimension=0, tiled...  620 us
    all_to_all x1, waiting for transfers between devices, layers_all_return_all(): jax.lax.all_to_all(frame_out, device_axis, concat_axis=0, split_axis=0)  101 us
    reduce_scatter x1, waiting for transfers between devices, body(): home = lax.psum_scatter(owners, 'cand', scatter_dimension=0, tiled=True)[0]  70.5 us
    ppermute x7, waiting for transfers between devices, shifted_2(): return lax.ppermute(value, axis, pairs)  56.1 us
    all_gather x1, blocking collectives, body(): everything = lax.all_gather(pooled[:, None], 'cand', axis=1, tiled=True)  36.7 us
  transfers between devices with their start and end apart: 12, of which 12 were waited for; matrix products, arithmetic and copies ran while one was open for 6% of the time, Pallas kernels for 0%

profile of v1, /device:TPU:0, one launch (start us, length us, event | category | flops | bytes accessed | tf_op | source)
XLA Modules:
  0.0 1746.4 jit_solution(14594481187534811226)
XLA Ops:
  7.2 5.2 stack.2
  12.4 11.7 all-to-all-start
  32.0 101.3 %all-to-all-done = bf16[128,32,1024]{2,1,0:T(8,128)(2,1)} async-done(((bf16[128,32,1024]{2,1,0:T(8,128)(2,1)}), bf16[128,32,1024]{2,1,0:T(8,128)(2,1)}, u32[]{:S(2)}, u32[]{:S(2)}) %all-to-all-start) | async-done | bytes 8388640 | tf_op jit(solution)/shard_map/all_to_all | solution.py:16
  133.3 4.7 convolution_convert_fusion
  143.4 6.1 collective-permute-done
  153.9 8.7 collective-permute-done.1
  167.2 9.8 collective-permute-done.2
  185.2 3.0 fusion.144
  188.2 7.4 collective-permute-done.3
  201.1 9.9 collective-permute-done.4
  218.8 2.9 fusion.140
  221.8 7.4 collective-permute-done.5
  234.7 6.7 collective-permute-done.6
  249.4 36.7 %all_gather.6 = f32[1,8,8,1024]{3,2,0,1:T(8,128)} all-gather(f32[1,1,8,1024]{3,2,0,1:T(8,128)S(1)} %select_add_fusion.1), channel_id=1, replica_groups=mesh['cand'=8,'prompt'=16] {'cand'}, dimensions={1}, use_global_device_ids=true | all-gather | bytes 294912 | tf_op jit(solution)/shard_map/all_gather | solution.py:94
  286.1 2.9 fusion.136
  289.1 11.1 all-gather.2.cloned.1.call-done
  300.2 4.4 select_reduce_fusion
  341.7 5.0 select_add_fusion
  346.8 5.9 fusion.77
  359.3 70.5 %reduce-scatter.6.cloned.1.call-done = f32[1,1,128,1024]{2,3,1,0:T(8,128)} async-done(((f32[8,1,128,1024]{2,3,1,0:T(8,128)}), f32[1,1,128,1024]{2,3,1,0:T(8,128)}) %reduce-scatter.6.cloned.1.call-update) | async-done | bytes 524304 | tf_op jit(solution)/shard_map/reduce_scatter | solution.py:160
  429.8 9.1 convolution_bitcast_fusion
  438.9 17.5 %copy.271 = f32[4096,1024]{1,0:T(8,128)} copy(f32[4096,1024]{0,1:T(8,128)} %convolution_bitcast_fusion) | data formatting | bytes 33554432
  456.4 619.8 %reduce-scatter.8.cloned.1.call-done = f32[8,1024]{1,0:T(8,128)} async-done(((f32[1024,1024]{1,0:T(8,128)}), f32[8,1024]{1,0:T(8,128)}) %reduce-scatter.8.cloned.1.call-update) | async-done | bytes 32784 | tf_op jit(solution)/shard_map/reduce_scatter | solution.py:117
  1076.2 663.4 %reduce-scatter.10.cloned.1.call-done = f32[32,1024]{1,0:T(8,128)} async-done(((f32[4096,1024]{1,0:T(8,128)}), f32[32,1024]{1,0:T(8,128)}) %reduce-scatter.10.cloned.1.call-update) | async-done | bytes 131088
  (417 shorter events, 89.3 us)
Async XLA Ops:
  7.2 126.1 %copy-start = (bf16[1,1,128,4096]{3,2,1,0:T(8,128)(2,1)S(1)}, bf16[1,1,128,4096]{3,2,1,0:T(8,128)(2,1)}, u32[]{:S(2)}) copy-start(bf16[1,1,128,4096]{3,2,1,0:T(8,128)(2,1)} %param.11) | copy-start | bytes 3145732
  12.4 120.9 %all-to-all-start = ((bf16[128,32,1024]{2,1,0:T(8,128)(2,1)}), bf16[128,32,1024]{2,1,0:T(8,128)(2,1)}, u32[]{:S(2)}, u32[]{:S(2)}) async-start(bf16[128,32,1024]{2,1,0:T(8,128)(2,1)} %stack.2), calls=%async_computation | async-start | bytes 16777216 | tf_op jit(solution)/shard_map/all_to_all | solution.py:16
  24.1 276.1 %all-gather.2.cloned.1.call-start = ((), (), s32[]{:S(2)}) async-start(), calls=%async_computation.4 | async-start | bytes 2113536 | tf_op jit(solution)/shard_map/all_gather | solution.py:95
  24.8 404.9 %reduce-scatter.6.cloned.1.call-start = ((), (), s32[]{:S(2)}) async-start(), calls=%async_computation.5 | async-start | bytes 4718592 | tf_op jit(solution)/shard_map/reduce_scatter | solution.py:160
  26.4 222.9 %copy-start.90 = (pred[8]{0:T(512)(128)(4,1)}, pred[8]{0:T(512)(128)(4,1)S(1)}, u32[]{:S(2)}) copy-start(pred[8]{0:T(512)(128)(4,1)S(1)} %iota_compare_fusion.16) | copy-start | bytes 28
  26.9 173.7 %copy-start.135 = (pred[128]{0:T(512)(128)(4,1)}, pred[128]{0:T(512)(128)(4,1)S(1)}, u32[]{:S(2)}) copy-start(pred[128]{0:T(512)(128)(4,1)S(1)} %iota_compare_fusion.15) | copy-start | bytes 388
  28.2 170.8 %copy-start.110 = (f32[128]{0:T(128)}, f32[128]{0:T(128)S(1)}, u32[]{:S(2)}) copy-start(f32[128]{0:T(128)S(1)} %select_divide_fusion) | copy-start | bytes 1540
  32.0 217.3 %copy-start.57 = (pred[8]{0:T(512)(128)(4,1)}, pred[8]{0:T(512)(128)(4,1)S(1)}, u32[]{:S(2)}) copy-start(pred[8]{0:T(512)(128)(4,1)S(1)} %get-tuple-element.62) | copy-start | bytes 28
  32.0 217.3 %copy-start.59 = (pred[8]{0:T(512)(128)(4,1)}, pred[8]{0:T(512)(128)(4,1)S(1)}, u32[]{:S(2)}) copy-start(pred[8]{0:T(512)(128)(4,1)S(1)} %get-tuple-element.63) | copy-start | bytes 28
  138.0 11.5 collective-permute-start
  143.2 106.1 %copy-start.61 = (pred[8]{0:T(512)(128)(4,1)}, pred[8]{0:T(512)(128)(4,1)S(1)}, u32[]{:S(2)}) copy-start(pred[8]{0:T(512)(128)(4,1)S(1)} %get-tuple-element.60) | copy-start | bytes 28
  143.2 106.1 %copy-start.63 = (pred[8]{0:T(512)(128)(4,1)}, pred[8]{0:T(512)(128)(4,1)S(1)}, u32[]{:S(2)}) copy-start(pred[8]{0:T(512)(128)(4,1)S(1)} %get-tuple-element.61) | copy-start | bytes 28
  143.2 106.1 %copy-start.65 = (pred[8]{0:T(512)(128)(4,1)}, pred[8]{0:T(512)(128)(4,1)S(1)}, u32[]{:S(2)}) copy-start(pred[8]{0:T(512)(128)(4,1)S(1)} %get-tuple-element.58) | copy-start | bytes 28
  143.2 106.1 %copy-start.67 = (pred[8]{0:T(512)(128)(4,1)}, pred[8]{0:T(512)(128)(4,1)S(1)}, u32[]{:S(2)}) copy-start(pred[8]{0:T(512)(128)(4,1)S(1)} %get-tuple-element.59) | copy-start | bytes 28
  152.0 10.6 collective-permute-start.1
  166.7 10.3 collective-permute-start.2
  184.5 11.1 collective-permute-start.3
  200.7 10.4 collective-permute-start.4
  218.6 10.6 collective-permute-start.5
  230.9 10.5 collective-permute-start.6
  244.6 44.4 %copy-start.49 = (f32[16,128]{1,0:T(8,128)}, f32[16,128]{1,0:T(8,128)S(1)}, u32[]{:S(2)}) copy-start(f32[16,128]{1,0:T(8,128)S(1)} %get-tuple-element.37) | copy-start | bytes 24580
  245.6 43.4 %copy-start.87 = (f32[16,128]{1,0:T(8,128)}, f32[16,128]{1,0:T(8,128)S(1)}, u32[]{:S(2)}) copy-start(f32[16,128]{1,0:T(8,128)S(1)} %fusion.58) | copy-start | bytes 24580
  346.7 729.5 %reduce-scatter.8.cloned.1.call-start = ((), (), s32[]{:S(2)}) async-start(), calls=%async_computation.6 | async-start | bytes 4227072 | tf_op jit(solution)/shard_map/reduce_scatter | solution.py:117
  352.8 1386.9 %reduce-scatter.10.cloned.1.call-start = ((), (), s32[]{:S(2)}) async-start(), calls=%async_computation.7 | async-start | bytes 16908288
  (126 other events, 496.2 us)
Sparse Core Ops, SparseCore 0:
  26.6 273.4 all-gather.1
  346.8 82.8 reduce-scatter.5
  432.8 643.3 reduce-scatter.7
  1079.0 660.5 reduce-scatter.9
